TPU v7x, 32 devices: a whole 2x2x4 slice. The times are simulated.
32 devices in a mesh: groups: 2 (over x), band: 16 (over z, y, core).
Axes of the slice: x: 2, y: 2, z: 4, core: 2. Of those that a mesh axis runs over, the one named last changes fastest.
Arguments:
- factor: bfloat16 [32768, 128], P(('groups', 'band')), parts along dimension 0
- near_vals: bfloat16 [512, 5, 64, 64], P(('groups', 'band')), parts along dimension 0, may hold values from 0.049804688 to 4
- far_vals: bfloat16 [32768, 512], P(('groups', 'band')), parts along dimension 0, may hold values from 0.049804688 to 4
- pub_rows: int32 [32, 32], P(('groups', 'band')), parts along dimension 0, may hold values from 0 to 1023
- far_count: int32 [32, 16], P(('groups', 'band')), parts along dimension 0, may hold values from 1 to 32, as said below
Outputs:
- updated: float32 [32768, 128], P(('groups', 'band')), parts along dimension 0
There are 2 independent parts, one for each index of `groups`. A program takes and returns all parts, laid end to end along the dimension named above; each array names one. Nothing has to cross between parts.
Inputs may be any that keep to these rules, and one draw needn't show every extreme that they name: `far_count`: in every row some entry equals 32.
All inputs are finite; a program needn't handle non-finite values.
Results may differ from a plain program's by a relative error of at most 0.0003.
Values may be sent and summed in bfloat16 or wider, within the bound.
A program may use at most 64 MiB of HBM per device.

v0:
```python
import jax
import jax.numpy as jnp
from jax import lax
from jax.sharding import PartitionSpec as P

BLOCK = 64
HALF_BLOCKS = 2


def extended(shard, sides, width):
    for axis, dim in sides:
        peers, length = (lax.axis_size(axis), shard.shape[dim])
        up = [(i, (i + 1) % peers) for i in range(peers - 1)]
        down = [(j, i) for i, j in up]
        last = lax.slice_in_dim(shard, length - width, length, axis=dim)
        first = lax.slice_in_dim(shard, 0, width, axis=dim)
        before = lax.ppermute(last, axis, up)
        after = lax.ppermute(first, axis, down)
        shard = jnp.concatenate([before, shard, after], axis=dim)
    return shard


def shards(factor, near_vals, far_vals, pub_rows, far_count):
    row_count, rank_width = factor.shape
    band_size = lax.axis_size("band")
    margin = HALF_BLOCKS * BLOCK
    padded = extended(factor, (("band", 0),), margin)
    block_count = row_count // BLOCK
    blocks = padded.reshape(block_count + 2 * HALF_BLOCKS, BLOCK, rank_width)
    near_sum = jnp.zeros((block_count, BLOCK, rank_width), jnp.float32)
    for offset in range(2 * HALF_BLOCKS + 1):
        near_sum = near_sum + jnp.einsum(
            "bij,bjk->bik",
            near_vals[:, offset],
            blocks[offset : offset + block_count],
            preferred_element_type=jnp.float32,
        )
    near_sum = near_sum.reshape(row_count, rank_width)
    slot_count = pub_rows.shape[1]
    chosen = jnp.take(factor, pub_rows[0], axis=0)
    slot_index = jnp.arange(band_size * slot_count, dtype=jnp.int32) % slot_count
    live_slots = slot_index < jnp.repeat(far_count[0], slot_count)
    masked = jnp.where(live_slots[None, :], far_vals, jnp.zeros((), far_vals.dtype))
    own_gram = lax.dot_general(
        factor, factor, (((0,), (0,)), ((), ())), preferred_element_type=jnp.float32
    )
    gram_matrix = lax.psum(own_gram, "band")
    arrived = lax.all_gather(chosen, "band", axis=0, tiled=True)
    far_sum = jnp.dot(masked, arrived, preferred_element_type=jnp.float32)
    lower_factor = jnp.linalg.cholesky(gram_matrix)
    inverse = jax.scipy.linalg.cho_solve(
        (lower_factor, True), jnp.eye(rank_width, dtype=jnp.float32)
    )
    return jnp.dot(near_sum + far_sum, inverse, precision=lax.Precision.HIGHEST)


def solution(mesh):
    placed = (
        P(("groups", "band"), None),
        P(("groups", "band"), None, None, None),
        P(("groups", "band"), None),
        P(("groups", "band"), None),
        P(("groups", "band"), None),
    )
    return jax.shard_map(
        shards, mesh=mesh, in_specs=placed, out_specs=P(("groups", "band"), None), check_vma=False
    )
```

profile of v0, /device:TPU:8, one launch (start us, length us, event | category | flops | bytes accessed | tf_op | source)
XLA Modules:
  0.0 138.6 jit_solution(12282025486069231995)
XLA Ops:
  6.5 0.0 copy-start
  6.5 0.0 all-reduce.2.cloned.1.call-start
  6.5 0.8 fusion.33
  7.4 1.9 %collective-permute-start = (bf16[128,128]{1,0:T(8,128)(2,1)S(1)}, bf16[128,128]{1,0:T(8,128)(2,1)S(1)}, u32[]{:S(2)}, u32[]{:S(2)}) collective-permute-start(bf16[128,128]{1,0:T(8,128)(2,1)S(1)} %get-tuple-element.11), channel_id=1, source_target_pairs={{0,1},{1,2},{2,3},{3,4},{4,5},{5,6},{6,7},{7,8},{8,9},{9,10},{10,1... | collective-permute-start | bytes 98312 | tf_op jit(solution)/shard_map/ppermute | solution.py:17
  9.3 4.5 %collective-permute-start.1 = (bf16[128,128]{1,0:T(8,128)(2,1)S(1)}, bf16[128,128]{1,0:T(8,128)(2,1)S(1)}, u32[]{:S(2)}, u32[]{:S(2)}) collective-permute-start(bf16[128,128]{1,0:T(8,128)(2,1)S(1)} %get-tuple-element.12), channel_id=1, source_target_pairs={{1,0},{2,1},{3,2},{4,3},{5,4},{6,5},{7,6},{8,7},{9,8},{10,9},{11,1... | collective-permute-start | bytes 98312 | tf_op jit(solution)/shard_map/ppermute | solution.py:18
  13.8 1.9 %fusion.34 = f32[128,128]{0,1:T(8,128)} fusion(bf16[1024,128]{1,0:T(8,128)(2,1)} %param.5), kind=kOutput, calls=%fused_computation.56 | convolution fusion | flops 33554432 | bytes 327680 | tf_op jit(solution)/shard_map/dot_general | solution.py:44
  15.8 0.0 all-reduce.2.cloned.1.call-update
  15.8 0.7 fusion.29
  16.5 0.7 compare_and_fusion
  17.1 1.6 %gather_fusion = bf16[32,128]{1,0:T(8,128)(2,1)S(1)} fusion(bf16[1024,128]{1,0:T(8,128)(2,1)} %param.5, s32[1024]{0:T(1024)S(1)} %pad_clamp_fusion), kind=kCustom, calls=%fused_computation | custom fusion | bytes 16512 | tf_op jit(solution)/shard_map/jit(_take)/gather | solution.py:40
  18.7 0.7 broadcast_in_dim.28
  19.4 0.1 reshape.74
  19.5 0.0 copy-start.1
  19.5 1.3 fusion.9
  20.9 0.1 broadcast_select_fusion
  20.9 19.7 %all_gather.3 = bf16[512,128]{1,0:T(8,128)(2,1)} all-gather(bf16[32,128]{1,0:T(8,128)(2,1)S(1)} %broadcast_select_fusion), channel_id=1, replica_groups=mesh['groups'=2,'band'=16] {'band'}, dimensions={0}, use_global_device_ids=true | all-gather | bytes 139264 | tf_op jit(solution)/shard_map/all_gather | solution.py:48
  40.6 0.0 collective-permute-done
  40.6 0.0 copy-done
  40.6 0.1 constant_dynamic-update-slice_fusion
  40.7 0.0 copy-done.1
  40.7 0.2 fusion.11
  40.9 0.0 collective-permute-done.1
  41.0 0.2 convolution_bitcast_fusion
  41.2 62.1 %all-reduce.2.cloned.1.call-done = f32[128,128]{0,1:T(8,128)} async-done(((f32[128,128]{0,1:T(8,128)}), f32[128,128]{0,1:T(8,128)}) %all-reduce.2.cloned.1.call-update) | async-done | bytes 65552 | tf_op jit(solution)/shard_map/psum | solution.py:47
  103.3 0.9 copy.12
  104.2 0.9 fusion.24
  105.1 11.7 %cholesky.17 = f32[128,128]{1,0:T(8,128)S(1)} custom-call(f32[128,128]{1,0:T(8,128)S(1)} %fusion.24), custom_call_target="Cholesky" | custom-call | tf_op jit(solution)/shard_map/jit(cholesky)/cholesky | solution.py:50
  116.8 0.6 compare_reduce_fusion
  117.5 0.7 fusion.19
  118.1 9.8 %custom-call.10 = f32[1,128,128]{1,2,0:T(8,128)S(1)} custom-call(f32[1,128,128]{2,1,0:T(8,128)S(1)} %fusion.19), custom_call_target="InvertDiagBlocksLowerTriangular" | custom-call | tf_op jit(solution)/shard_map/jit(_cho_solve)/triangular_solve | solution.py:51
  128.0 0.2 fusion.22
  128.2 0.2 fusion.20
  128.4 0.2 fusion.3
  128.6 0.0 copy-start.2
  128.7 0.0 copy-start.3
  128.7 0.2 fusion.1
  128.9 0.7 copy-done.2
  129.6 0.4 copy-done.3
  130.0 0.4 convolution_add_fusion
  130.4 1.4 fusion.35
  (7 shorter events, 0.1 us)
Async XLA Ops:
  6.5 34.1 %copy-start = (bf16[1024,128]{1,0:T(8,128)(2,1)S(1)}, bf16[1024,128]{1,0:T(8,128)(2,1)}, u32[]{:S(2)}) copy-start(bf16[1024,128]{1,0:T(8,128)(2,1)} %param.5) | copy-start | bytes 786436
  6.5 96.8 %all-reduce.2.cloned.1.call-start = ((), (), s32[]{:S(2)}) async-start(), calls=%async_computation | async-start | bytes 131072 | tf_op jit(solution)/shard_map/psum | solution.py:47
  7.4 33.2 %collective-permute-start = (bf16[128,128]{1,0:T(8,128)(2,1)S(1)}, bf16[128,128]{1,0:T(8,128)(2,1)S(1)}, u32[]{:S(2)}, u32[]{:S(2)}) collective-permute-start(bf16[128,128]{1,0:T(8,128)(2,1)S(1)} %get-tuple-element.11), channel_id=1, source_target_pairs={{0,1},{1,2},{2,3},{3,4},{4,5},{5,6},{6,7},{7,8},{8,9},{9,10},{10,1... | collective-permute-start | bytes 98312 | tf_op jit(solution)/shard_map/ppermute | solution.py:17
  9.3 31.7 %collective-permute-start.1 = (bf16[128,128]{1,0:T(8,128)(2,1)S(1)}, bf16[128,128]{1,0:T(8,128)(2,1)S(1)}, u32[]{:S(2)}, u32[]{:S(2)}) collective-permute-start(bf16[128,128]{1,0:T(8,128)(2,1)S(1)} %get-tuple-element.12), channel_id=1, source_target_pairs={{1,0},{2,1},{3,2},{4,3},{5,4},{6,5},{7,6},{8,7},{9,8},{10,9},{11,1... | collective-permute-start | bytes 98312 | tf_op jit(solution)/shard_map/ppermute | solution.py:18
  19.5 21.2 %copy-start.1 = (bf16[16,5,64,64]{3,2,1,0:T(8,128)(2,1)S(1)}, bf16[16,5,64,64]{3,2,1,0:T(8,128)(2,1)}, u32[]{:S(2)}) copy-start(bf16[16,5,64,64]{3,2,1,0:T(8,128)(2,1)} %param.6) | copy-start | bytes 1966084
  128.6 0.9 copy-start.2
  128.7 1.3 copy-start.3
Sparse Core Ops, SparseCore 0:
  15.9 87.3 all-reduce.1
where the time goes:
time: 139 us
  waiting for transfers between devices  62.1 us (45%)
  other arithmetic  25.1 us (18%)
  blocking collectives  19.7 us (14%)
  between operations  13.5 us (10%)
  starting transfers between devices  6.45 us (5%)
  matrix products  6.39 us (5%)
  local copies, waits for them, and re-layouts  5.35 us (4%)
    psum x1, waiting for transfers between devices, shards(): gram_matrix = lax.psum(own_gram, 'band')  62.1 us
    all_gather x1, blocking collectives, shards(): arrived = lax.all_gather(chosen, 'band', axis=0, tiled=True)  19.7 us
    another operation x3, other arithmetic, shards(): lower_factor = jnp.linalg.cholesky(gram_matrix)  12.4 us
    another operation x2, other arithmetic, shards(): jax.scipy.linalg.cho_solve((lower_factor, True), jnp.eye(rank_width, dtyp...  10.5 us
    ppermute x1, starting transfers between devices, extended(): after = lax.ppermute(first, axis, down)  4.54 us
  transfers between devices with their start and end apart: 3, of which 1 were waited for; matrix products, arithmetic and copies ran while one was open for 6% of the time, Pallas kernels for 0%

commit v1 on v0

--- a/solution.py
+++ b/solution.py
@@ -1,3 +1,4 @@
+import functools
 import jax
 import jax.numpy as jnp
 from jax import lax
@@ -5,6 +6,13 @@
 
 BLOCK = 64
 HALF_BLOCKS = 2
+
+
+def _edit_sources_all(field, axis_id):
+    return jnp.sum(lax.all_gather(field, axis_id), axis=0)
+
+
+fields_mark = functools.partial(_edit_sources_all, axis_id="band")
 
 
 def extended(shard, sides, width):
@@ -44,7 +52,7 @@
     own_gram = lax.dot_general(
         factor, factor, (((0,), (0,)), ((), ())), preferred_element_type=jnp.float32
     )
-    gram_matrix = lax.psum(own_gram, "band")
+    gram_matrix = fields_mark(own_gram)
     arrived = lax.all_gather(chosen, "band", axis=0, tiled=True)
     far_sum = jnp.dot(masked, arrived, preferred_element_type=jnp.float32)
     lower_factor = jnp.linalg.cholesky(gram_matrix)

time: 139 us -> 89 us (0.64)
  the two profiles are of different devices: /device:TPU:8 before, /device:TPU:0 now
where the time goes in v1:
time: 89 us; the launch traced here: 88.6 us
  other arithmetic  25.6 us (29%)
  blocking collectives  25.4 us (29%)
  between operations  13.5 us (15%)
  waiting for transfers between devices  8.67 us (10%)
  matrix products  6.27 us (7%)
  local copies, waits for them, and re-layouts  5.58 us (6%)
  starting transfers between devices  3.64 us (4%)
    all_gather x1, blocking collectives, shards(): arrived = lax.all_gather(chosen, 'band', axis=0, tiled=True)  25.4 us
    another operation x3, other arithmetic, shards(): lower_factor = jnp.linalg.cholesky(gram_matrix)  12.4 us
    another operation x2, other arithmetic, shards(): jax.scipy.linalg.cho_solve((lower_factor, True), jnp.eye(rank_width, dtyp...  10.5 us
    all_gather x1, waiting for transfers between devices, _edit_sources_all(): return jnp.sum(lax.all_gather(field, axis_id), axis=0)  8.64 us
    ppermute x1, starting transfers between devices, extended(): before = lax.ppermute(last, axis, up)  2.35 us
    unnamed x7, local copies, waits for them, and re-layouts  2.15 us
    dot_general x5, matrix products, shards(): jnp.einsum('bij,bjk->bik', near_vals[:, offset], blocks[offset:offset + b...  2.09 us
    dot_general x1, matrix products, shards(): lax.dot_general(factor, factor, (((0,), (0,)), ((), ())), preferred_eleme...  1.93 us
  transfers between devices with their start and end apart: 3, of which 1 were waited for; matrix products, arithmetic and copies ran while one was open for 9% of the time, Pallas kernels for 0%

profile of v1, /device:TPU:0, one launch (start us, length us, event | category | flops | bytes accessed | tf_op | source)
XLA Modules:
  0.0 88.6 jit_solution(13593330854863612922)
XLA Ops:
  6.5 0.0 copy-start
  6.5 0.0 all-gather.3.cloned.1.call-start
  6.5 0.8 fusion.33
  7.4 2.3 %collective-permute-start = (bf16[128,128]{1,0:T(8,128)(2,1)S(1)}, bf16[128,128]{1,0:T(8,128)(2,1)S(1)}, u32[]{:S(2)}, u32[]{:S(2)}) collective-permute-start(bf16[128,128]{1,0:T(8,128)(2,1)S(1)} %get-tuple-element.11), channel_id=1, source_target_pairs={{0,1},{1,2},{2,3},{3,4},{4,5},{5,6},{6,7},{7,8},{8,9},{9,10},{10,1... | collective-permute-start | bytes 98312 | tf_op jit(solution)/shard_map/ppermute | solution.py:25
  9.7 1.3 %collective-permute-start.1 = (bf16[128,128]{1,0:T(8,128)(2,1)S(1)}, bf16[128,128]{1,0:T(8,128)(2,1)S(1)}, u32[]{:S(2)}, u32[]{:S(2)}) collective-permute-start(bf16[128,128]{1,0:T(8,128)(2,1)S(1)} %get-tuple-element.12), channel_id=1, source_target_pairs={{1,0},{2,1},{3,2},{4,3},{5,4},{6,5},{7,6},{8,7},{9,8},{10,9},{11,1... | collective-permute-start | bytes 98312 | tf_op jit(solution)/shard_map/ppermute | solution.py:26
  11.0 1.9 %fusion.34 = f32[128,128]{1,0:T(8,128)} fusion(bf16[1024,128]{1,0:T(8,128)(2,1)} %param.5), kind=kOutput, calls=%fused_computation.56 | convolution fusion | flops 33554432 | bytes 327680 | tf_op jit(solution)/shard_map/dot_general | solution.py:52
  13.0 0.0 all-gather.3.cloned.1.call-update
  13.0 0.7 fusion.29
  13.6 0.7 compare_and_fusion
  14.3 1.6 %gather_fusion = bf16[32,128]{1,0:T(8,128)(2,1)S(1)} fusion(bf16[1024,128]{1,0:T(8,128)(2,1)} %param.5, s32[1024]{0:T(1024)S(1)} %pad_clamp_fusion), kind=kCustom, calls=%fused_computation | custom fusion | bytes 16512 | tf_op jit(solution)/shard_map/jit(_take)/gather | solution.py:48
  15.9 0.7 broadcast_in_dim.28
  16.6 0.1 reshape.74
  16.7 1.2 %fusion.9 = f32[16,64,128]{2,1,0:T(8,128)S(1)} fusion(bf16[16,64,128]{2,1,0:T(8,128)(2,1)} %bitcast.73, bf16[16,5,64,64]{3,2,1,0:T(8,128)(2,1)} %param.6), kind=kOutput, calls=%fused_computation.14 | convolution fusion | flops 16777216 | bytes 1048576 | tf_op jit(solution)/shard_map/bij,bjk->bik/dot_general | solution.py:40
  17.9 0.1 broadcast_select_fusion
  18.0 25.4 %all_gather.9 = bf16[512,128]{1,0:T(8,128)(2,1)S(1)} all-gather(bf16[32,128]{1,0:T(8,128)(2,1)S(1)} %broadcast_select_fusion), channel_id=1, replica_groups=mesh['groups'=2,'band'=16] {'band'}, dimensions={0}, use_global_device_ids=true | all-gather | bytes 139264 | tf_op jit(solution)/shard_map/all_gather | solution.py:56
  43.4 0.0 collective-permute-done
  43.4 0.0 copy-done
  43.4 0.0 copy-start.1
  43.4 0.1 constant_dynamic-update-slice_fusion
  43.5 0.0 collective-permute-done.1
  43.6 1.1 %copy-done.1 = bf16[16,5,64,64]{3,2,1,0:T(8,128)(2,1)S(1)} copy-done((bf16[16,5,64,64]{3,2,1,0:T(8,128)(2,1)S(1)}, bf16[16,5,64,64]{3,2,1,0:T(8,128)(2,1)}, u32[]{:S(2)}) %copy-start.1) | copy-done | bytes 655384
  44.7 0.2 fusion.11
  44.9 0.2 convolution_bitcast_fusion
  45.2 0.2 fusion.3
  45.4 0.0 copy-start.2
  45.4 0.2 fusion.1
  45.6 1.0 %copy-done.2 = bf16[1024,512]{1,0:T(8,128)(2,1)S(1)} copy-done((bf16[1024,512]{1,0:T(8,128)(2,1)S(1)}, bf16[1024,512]{1,0:T(8,128)(2,1)}, u32[]{:S(2)}) %copy-start.2) | copy-done | bytes 1048600
  46.6 0.4 convolution_add_fusion
  47.0 8.6 %all-gather.3.cloned.1.call-done = f32[2048,128]{1,0:T(8,128)} async-done(((f32[128,128]{1,0:T(8,128)}), f32[2048,128]{1,0:T(8,128)}) %all-gather.3.cloned.1.call-update) | async-done | bytes 1048592 | tf_op jit(solution)/shard_map/all_gather | solution.py:12
  55.7 1.3 %reduce_sum.9 = f32[128,128]{1,0:T(8,128)S(1)} reduce(f32[16,128,128]{2,1,0:T(8,128)} %bitcast.74, f32[]{:T(128)} %constant.79.clone.1), dimensions={0}, to_apply=%region_0.1 | reduce | flops 245760 | bytes 1114116 | tf_op jit(solution)/shard_map/reduce_sum | solution.py:12
  57.0 0.1 copy.17
  57.1 11.7 %cholesky.17 = f32[128,128]{1,0:T(8,128)S(1)} custom-call(f32[128,128]{1,0:T(8,128)S(1)} %fusion.24), custom_call_target="Cholesky" | custom-call | tf_op jit(solution)/shard_map/jit(cholesky)/cholesky | solution.py:58
  68.8 0.6 compare_reduce_fusion
  69.5 0.7 fusion.19
  70.2 9.8 %custom-call.10 = f32[1,128,128]{1,2,0:T(8,128)S(1)} custom-call(f32[1,128,128]{2,1,0:T(8,128)S(1)} %fusion.19), custom_call_target="InvertDiagBlocksLowerTriangular" | custom-call | tf_op jit(solution)/shard_map/jit(_cho_solve)/triangular_solve | solution.py:59
  80.0 0.2 fusion.22
  80.2 0.2 fusion.20
  80.4 1.4 %fusion.35 = f32[1024,128]{1,0:T(8,128)} fusion(f32[1024,128]{1,0:T(8,128)S(1)} %convolution_add_fusion, f32[128,128]{1,0:T(8,128)S(1)} %fusion.20), kind=kOutput, calls=%fused_computation.57 | convolution fusion | flops 201326592 | bytes 1114112 | tf_op jit(solution)/shard_map/dot_general | solution.py:62
  (8 shorter events, 0.1 us)
Async XLA Ops:
  6.5 36.9 %copy-start = (bf16[1024,128]{1,0:T(8,128)(2,1)S(1)}, bf16[1024,128]{1,0:T(8,128)(2,1)}, u32[]{:S(2)}) copy-start(bf16[1024,128]{1,0:T(8,128)(2,1)} %param.5) | copy-start | bytes 786436
  6.5 49.2 %all-gather.3.cloned.1.call-start = ((), (), s32[]{:S(2)}) async-start(), calls=%async_computation | async-start | bytes 1114112 | tf_op jit(solution)/shard_map/all_gather | solution.py:12
  7.4 36.0 %collective-permute-start = (bf16[128,128]{1,0:T(8,128)(2,1)S(1)}, bf16[128,128]{1,0:T(8,128)(2,1)S(1)}, u32[]{:S(2)}, u32[]{:S(2)}) collective-permute-start(bf16[128,128]{1,0:T(8,128)(2,1)S(1)} %get-tuple-element.11), channel_id=1, source_target_pairs={{0,1},{1,2},{2,3},{3,4},{4,5},{5,6},{6,7},{7,8},{8,9},{9,10},{10,1... | collective-permute-start | bytes 98312 | tf_op jit(solution)/shard_map/ppermute | solution.py:25
  9.7 33.8 %collective-permute-start.1 = (bf16[128,128]{1,0:T(8,128)(2,1)S(1)}, bf16[128,128]{1,0:T(8,128)(2,1)S(1)}, u32[]{:S(2)}, u32[]{:S(2)}) collective-permute-start(bf16[128,128]{1,0:T(8,128)(2,1)S(1)} %get-tuple-element.12), channel_id=1, source_target_pairs={{1,0},{2,1},{3,2},{4,3},{5,4},{6,5},{7,6},{8,7},{9,8},{10,9},{11,1... | collective-permute-start | bytes 98312 | tf_op jit(solution)/shard_map/ppermute | solution.py:26
  43.4 1.3 %copy-start.1 = (bf16[16,5,64,64]{3,2,1,0:T(8,128)(2,1)S(1)}, bf16[16,5,64,64]{3,2,1,0:T(8,128)(2,1)}, u32[]{:S(2)}) copy-start(bf16[16,5,64,64]{3,2,1,0:T(8,128)(2,1)} %param.6) | copy-start | bytes 1966084
  45.4 1.2 %copy-start.2 = (bf16[1024,512]{1,0:T(8,128)(2,1)S(1)}, bf16[1024,512]{1,0:T(8,128)(2,1)}, u32[]{:S(2)}) copy-start(bf16[1024,512]{1,0:T(8,128)(2,1)} %param.7) | copy-start | bytes 3145732
Sparse Core Ops, SparseCore 0:
  13.1 42.5 all-gather.2
